TPU v7x, 32 devices: a whole 2x2x4 slice. The times are simulated.
32 devices in a mesh: grp: 2 (over y), wide: 4 (over z), patch: 2 (over x), sub: 2 (over core).
Axes of the slice: x: 2, y: 2, z: 4, core: 2. Of those that a mesh axis runs over, the one named last changes fastest.
Arguments:
- survey: bfloat16 [512, 20, 729], P('wide', ('grp', 'patch')), parts along dimension 1, may hold values from -34 to 34
- test_matrix: bfloat16 [625, 48], replicated, may hold values from -6 to 6
Outputs:
- restored: float32 [512, 20, 729], P('wide', ('grp', 'patch')), parts along dimension 1
There are 2 independent parts, one for each index of `grp`. A program takes and returns all parts, laid end to end along the dimension named above; an argument that names none is the same for every part. Nothing has to cross between parts.
All inputs are finite; a program needn't handle non-finite values.
Results may differ from a plain program's by a relative error of at most 0.0014.
Values may be sent and summed in bfloat16 or wider, within the bound.
A program may use at most 64 MiB of HBM per device.

v0:
```python
import math

import jax
import jax.numpy as jnp
from jax import lax
from jax.sharding import PartitionSpec as P

LH = 5
RANK = 48
FD = 1
PS = 9
ORDER = 625
TR3 = 729


DAMP = 0.5
HIGHEST = lax.Precision.HIGHEST
block_group = 3


def shifted_2(x, axis, by):
    devices = lax.axis_size(axis)
    return lax.ppermute(x, axis, [(i, (i + by) % devices) for i in range(devices)])


def level_weight():
    planes = jnp.arange(PS, dtype=jnp.int32)
    return jnp.minimum(jnp.minimum(planes + 1, PS - planes), LH).astype(jnp.float32)


def average_counts():
    weight = level_weight()
    return (
        weight[:, None, None, None]
        * weight[None, :, None, None]
        * weight[None, None, :, None]
        * weight[None, None, None, :]
    )


def phases(time_total, freq_total):
    frequency = jnp.arange(freq_total, dtype=jnp.int32) + 1
    moments = jnp.arange(time_total, dtype=jnp.int32)
    turned = frequency[:, None] * moments[None, :] % time_total
    return turned.astype(jnp.float32) * (2.0 * math.pi / time_total)


def forward_table(time_total, freq_total):
    angles = phases(time_total, freq_total)
    factor = 1.0 / math.sqrt(time_total)
    matrix = jnp.stack([jnp.cos(angles) * factor, -jnp.sin(angles) * factor], 1)
    return matrix.reshape(2 * freq_total, time_total).astype(jnp.bfloat16)


def inverse_table(time_total, freq_total):
    angles = phases(time_total, freq_total)
    factor = 2.0 / math.sqrt(time_total)
    matrix = jnp.stack([jnp.cos(angles) * factor, -jnp.sin(angles) * factor], 1)
    return matrix.reshape(2 * freq_total, time_total)


def gram_of(matrix):
    return lax.dot_general(
        matrix,
        matrix,
        (((1,), (1,)), ((), ())),
        precision=HIGHEST,
        preferred_element_type=jnp.float32,
    )


def hankel_columns(slab_data):
    level_three = jnp.stack(
        [slab_data[:, :, :, offset : offset + LH, :] for offset in range(LH)], 0
    )
    level_four = jnp.stack([level_three[..., offset : offset + LH] for offset in range(LH)], 1)
    return level_four.reshape(LH * LH, 2 * ORDER)


def reduce_frequency(spectrum, test_matrix):
    member = lax.axis_index("sub")
    members = lax.axis_size("sub")
    block_width = LH * LH
    per_member = -(-block_width // members)
    turn_count = -(-per_member // block_group)
    anchor = jnp.zeros((), jnp.int32)
    unused_value, pullback = jax.vjp(hankel_columns, jnp.zeros((2, LH, LH, PS, PS), jnp.float32))

    def places_of(turn_index):
        places = []
        for within in range(block_group):
            local_block = turn_index * block_group + within
            global_block = member * per_member + local_block
            usable = jnp.logical_and(local_block < per_member, global_block < block_width)
            clamped_block = jnp.minimum(global_block, block_width - 1)
            places.append((clamped_block, usable))
        return places

    def blocks_of(turn_index):
        places = places_of(turn_index)
        hankels = []
        for clamped_block, usable in places:
            corner = (anchor, clamped_block // LH, clamped_block % LH, anchor, anchor)
            built_block = hankel_columns(lax.dynamic_slice(spectrum, corner, (2, LH, LH, PS, PS)))
            hankels.append(jnp.where(usable, built_block, jnp.zeros_like(built_block)))
        return (jnp.concatenate(hankels, 0), places)

    def sketch_turn(turn_index, partial_sum):
        hankel, places = blocks_of(turn_index)
        test_rows = jnp.concatenate(
            [
                lax.dynamic_slice_in_dim(test_matrix, clamped_block * block_width, block_width, 0)
                for clamped_block, usable in places
            ],
            0,
        )
        return partial_sum + lax.dot_general(
            test_rows, hankel, (((0,), (0,)), ((), ())), preferred_element_type=jnp.float32
        )

    sketch = lax.fori_loop(0, turn_count, sketch_turn, jnp.zeros((RANK, 2 * ORDER), jnp.float32))
    sketch = lax.psum(sketch, "sub")
    basis_rows = jnp.concatenate(
        [sketch, jnp.concatenate([-sketch[:, ORDER:], sketch[:, :ORDER]], 1)], 0
    )
    gram_matrix = gram_of(basis_rows)
    factor = jnp.linalg.cholesky(gram_matrix)
    orthonormal = jax.scipy.linalg.solve_triangular(factor, basis_rows, lower=True).astype(
        jnp.bfloat16
    )
    paired = jnp.concatenate(
        [orthonormal, jnp.concatenate([orthonormal[:, ORDER:], -orthonormal[:, :ORDER]], 1)], 0
    )

    def coupling_turn(turn_index, carried_state):
        damping, stored = carried_state
        hankel, places = blocks_of(turn_index)
        products = lax.dot_general(
            paired, hankel, (((1,), (1,)), ((), ())), preferred_element_type=jnp.float32
        )
        direct = products[: 2 * RANK]
        twisted = products[2 * RANK :]
        damping = damping + gram_of(direct) + gram_of(twisted)
        stored = lax.dynamic_update_slice_in_dim(stored, direct[None], turn_index, 0)
        return (damping, stored)

    start_state = (
        jnp.zeros((2 * RANK, 2 * RANK), jnp.float32),
        jnp.zeros((turn_count, 2 * RANK, block_group * block_width), jnp.float32),
    )
    damping, stored = lax.fori_loop(0, turn_count, coupling_turn, start_state)
    damping = lax.psum(damping, "sub")
    damp_level = DAMP * jnp.trace(damping) / (2 * RANK)
    shifted = damping + damp_level * jnp.eye(2 * RANK, dtype=jnp.float32)
    kernel = jax.scipy.linalg.cho_solve((jnp.linalg.cholesky(shifted), True), damping)
    coeffs = jnp.einsum("rs,tsj->trj", kernel, stored, precision=HIGHEST).astype(jnp.bfloat16)

    def rebuild_turn(turn_index, totals):
        block_coeff = lax.dynamic_index_in_dim(coeffs, turn_index, 0, keepdims=False)
        rebuilt = lax.dot_general(
            block_coeff, orthonormal, (((0,), (0,)), ((), ())), preferred_element_type=jnp.float32
        )
        places = places_of(turn_index)
        for within in range(block_group):
            clamped_block = places[within][0]
            piece_rows = rebuilt[within * block_width : (within + 1) * block_width]
            slab_grad = pullback(piece_rows)[0]
            corner = (anchor, clamped_block // LH, clamped_block % LH, anchor, anchor)
            current = lax.dynamic_slice(totals, corner, (2, LH, LH, PS, PS))
            totals = lax.dynamic_update_slice(totals, current + slab_grad, corner)
        return totals

    totals = lax.fori_loop(0, turn_count, rebuild_turn, jnp.zeros((2, PS, PS, PS, PS), jnp.float32))
    totals = lax.psum(totals, "sub")
    return totals / average_counts()


def forward_transform(planes, wide_count):
    time_local, plane_count, unused_size = planes.shape
    traces = plane_count * TR3
    per_device = -(-traces // wide_count)
    flat_rows = planes.reshape(time_local, traces)
    flat_rows = jnp.pad(flat_rows, ((0, 0), (0, per_device * wide_count - traces)))
    columns = lax.all_to_all(flat_rows, "wide", split_axis=1, concat_axis=0, tiled=True)
    transform = forward_table(time_local * wide_count, FD * wide_count)
    spectra = jnp.dot(transform, columns, preferred_element_type=jnp.float32).astype(jnp.bfloat16)
    spectra = spectra.reshape(FD * wide_count, 2, per_device)
    own_freqs = lax.all_to_all(spectra, "wide", split_axis=0, concat_axis=2, tiled=True)
    return own_freqs[:, :, :traces].reshape(FD, 2, plane_count, TR3)


def inverse_transform(smooth, wide_count, time_local):
    plane_count = smooth.shape[2]
    traces = plane_count * TR3
    per_device = -(-traces // wide_count)
    flat_rows = smooth.reshape(FD, 2, traces)
    flat_rows = jnp.pad(flat_rows, ((0, 0), (0, 0), (0, per_device * wide_count - traces)))
    gathered = lax.all_to_all(flat_rows, "wide", split_axis=2, concat_axis=0, tiled=True)
    transform = inverse_table(time_local * wide_count, FD * wide_count)
    series = lax.dot_general(
        transform,
        gathered.reshape(2 * FD * wide_count, per_device),
        (((0,), (0,)), ((), ())),
        precision=HIGHEST,
        preferred_element_type=jnp.float32,
    )
    local_rows = lax.all_to_all(series, "wide", split_axis=0, concat_axis=1, tiled=True)
    return local_rows[:, :traces].reshape(time_local, plane_count, TR3)


def shards(survey, test_matrix):
    wide_count = lax.axis_size("wide")
    time_local = survey.shape[0]
    rim_planes = shifted_2(survey[:, : LH - 1, :], "patch", -1)
    planes = jnp.concatenate([survey, rim_planes], 1)
    spectra = forward_transform(planes, wide_count)
    grid_data = spectra.reshape(FD, 2, PS, PS, PS, PS)
    averaged = jnp.stack([reduce_frequency(grid_data[0], test_matrix)], 0)
    weights = level_weight() / LH
    smooth = averaged.reshape(FD, 2, PS, TR3) * weights[None, None, :, None]
    carried = shifted_2(smooth[:, :, LH:, :], "patch", 1)
    smooth = jnp.concatenate([smooth[:, :, : LH - 1, :] + carried, smooth[:, :, LH - 1 : LH, :]], 2)
    result = inverse_transform(smooth, wide_count, time_local)
    return result


def solution(mesh):
    return jax.shard_map(
        shards,
        mesh=mesh,
        in_specs=(P("wide", ("grp", "patch"), None), P()),
        out_specs=P("wide", ("grp", "patch"), None),
        check_vma=False,
    )
```

profile of v0, /device:TPU:0, one launch (start us, length us, event | category | flops | bytes accessed | tf_op | source)
XLA Modules:
  0.0 681.2 jit_solution(15878286249713786575)
XLA Ops:
  7.7 3.0 collective-permute-start
  10.7 16.8 %collective-permute-done = bf16[128,4,729]{0,2,1:T(8,128)(2,1)S(1)} collective-permute-done((bf16[128,4,729]{0,2,1:T(8,128)(2,1)S(1)}, bf16[128,4,729]{0,2,1:T(8,128)(2,1)S(1)}, u32[]{:S(2)}, u32[]{:S(2)}) %collective-permute-start) | collective-permute-done | bytes 746528 | tf_op jit(solution)/shard_map/ppermute | solution.py:23
  33.7 5.1 all-to-all-start
  40.4 36.9 %all-to-all-done = bf16[128,4,1641]{0,2,1:T(8,128)(2,1)S(1)} async-done(((bf16[128,4,1641]{0,2,1:T(8,128)(2,1)}), bf16[128,4,1641]{0,2,1:T(8,128)(2,1)S(1)}, u32[]{:S(2)}, u32[]{:S(2)}) %all-to-all-start) | async-done | bytes 1680416 | tf_op jit(solution)/shard_map/all_to_all | solution.py:184
  82.3 3.3 all-to-all-start.1
  86.3 4.8 all-to-all-done.1
  91.7 143.4 %while.53 = (s32[]{:T(128)}, f32[48,1250]{1,0:T(8,128)S(1)}, s32[]{:T(128)}, bf16[625,48]{0,1:T(8,128)(2,1)}, bf16[2,9,9,9,9]{4,3,2,1,0:T(8,128)(2,1)S(1)}, /*in...) while((s32[]{:T(128)}, f32[48,1250]{1,0:T(8,128)S(1)}, ...), condition=%wide.region_1.2_spmd.clone, body=%wide.region_0.1_spmd.clone.sunk | while | flops 9797941 | bytes 17153020 | solution.py:121
  101.2 3.2 select_n.853
  130.5 3.2 select_n.853
  159.8 3.2 select_n.853
  189.1 3.2 select_n.853
  218.4 3.2 select_n.853
  237.8 14.7 %all-reduce.34.cloned.1.call-done = f32[48,1250]{1,0:T(8,128)} async-done(((f32[48,1250]{1,0:T(8,128)}), f32[48,1250]{1,0:T(8,128)}) %all-reduce.34.cloned.1.call-update) | async-done | bytes 240016 | tf_op jit(solution)/shard_map/psum | solution.py:122
  255.4 8.8 %cholesky.44 = f32[96,96]{1,0:T(8,128)S(1)} custom-call(f32[96,96]{1,0:T(8,128)S(1)} %fusion.96), custom_call_target="Cholesky" | custom-call | tf_op jit(solution)/shard_map/jit(cholesky)/cholesky | solution.py:127
  265.4 7.4 %custom-call.13 = f32[1,96,96]{1,2,0:T(8,128)S(1)} custom-call(f32[1,96,96]{2,1,0:T(8,128)S(1)} %fusion.89), custom_call_target="InvertDiagBlocksLowerTriangular" | custom-call | tf_op jit(solution)/shard_map/jit(_solve_triangular)/triangular_solve | solution.py:128
  275.3 151.4 %while.54 = (s32[]{:T(128)}, f32[96,96]{1,0:T(8,128)}, f32[5,96,75]{1,2,0:T(8,128)}, s32[]{:T(128)}, bf16[2,9,9,9,9]{4,3,2,1,0:T(8,128)(2,1)S(1)}, /*index=5*/bf...) while((s32[]{:T(128)}, f32[96,96]{1,0:T(8,128)}, ...), condition=%wide.region_6.8_spmd.clone, body=%wide.region_5.7_spmd.clone.sunk | while | flops 53272776 | bytes 17500804 | solution.py:151
  284.8 3.2 select_n.877
  315.1 3.2 select_n.877
  346.3 3.2 select_n.877
  377.4 3.2 select_n.877
  408.5 3.2 select_n.877
  426.8 4.3 psum.22
  432.5 8.8 %cholesky.55 = f32[96,96]{1,0:T(8,128)S(1)} custom-call(f32[96,96]{1,0:T(8,128)S(1)} %copy.135), custom_call_target="Cholesky" | custom-call | tf_op jit(solution)/shard_map/jit(cholesky)/cholesky | solution.py:155
  442.6 7.4 %custom-call.14 = f32[1,96,96]{1,2,0:T(8,128)S(1)} custom-call(f32[1,96,96]{2,1,0:T(8,128)S(1)} %fusion.90), custom_call_target="InvertDiagBlocksLowerTriangular" | custom-call | tf_op jit(solution)/shard_map/jit(_cho_solve)/triangular_solve | solution.py:155
  451.7 125.5 %while.52 = (s32[]{:T(128)}, f32[2,9,9,9,9]{4,3,2,1,0:T(8,128)S(1)}, s32[]{:T(128)}, bf16[5,96,75]{1,2,0:T(8,128)(2,1)S(1)}, bf16[96,1250]{1,0:T(8,128)(2,1)S(1)...) while((s32[]{:T(128)}, ...), condition=%wide.region_10.12_spmd, body=%wide.region_9.11_spmd.sunk | while | flops 18195776 | bytes 9201650 | solution.py:173
  452.0 4.0 reshape.416
  456.0 2.8 slice_bitcast_fusion.66
  460.3 4.0 reshape.417
  464.3 2.8 slice_bitcast_fusion.68
  468.6 4.0 reshape.418
  477.1 4.0 reshape.416
  485.4 4.0 reshape.417
  493.7 4.0 reshape.418
  502.2 4.0 reshape.416
  510.5 4.0 reshape.417
  518.8 4.0 reshape.418
  527.3 4.0 reshape.416
  535.6 4.0 reshape.417
  543.9 4.0 reshape.418
  552.5 4.0 reshape.416
  560.7 4.0 reshape.417
  569.0 4.0 reshape.418
  577.3 6.5 psum.23
  590.8 2.8 pad_bitcast_fusion
  594.1 17.1 %reduce.4 = f32[3648,2]{1,0:T(8,128)S(1)} reduce(f32[3648,1,2]{2,1,0:T(1,128)} %pad_bitcast_fusion, f32[]{:T(128)} %broadcast.600), dimensions={1}, to_apply=%pad_bitcast_fusion.reduce_sub_computation | reduce | bytes 58372
  612.9 4.8 all-to-all-start.2
  617.8 5.6 all-to-all-done.2
  629.0 43.8 %all_to_all.68 = f32[4,128,912]{1,2,0:T(8,128)S(1)} all-to-all(f32[4,128,912]{1,2,0:T(8,128)S(1)} %fusion.101), channel_id=1, replica_groups=mesh['grp'=2,'wide'=4,'patch'=2,'sub'=2] {'wide'}, dimensions={0} | all-to-all | bytes 3735552 | tf_op jit(solution)/shard_map/all_to_all | solution.py:207
  (502 shorter events, 364.3 us)
Async XLA Ops:
  7.7 19.8 %collective-permute-start = (bf16[128,4,729]{0,2,1:T(8,128)(2,1)S(1)}, bf16[128,4,729]{0,2,1:T(8,128)(2,1)S(1)}, u32[]{:S(2)}, u32[]{:S(2)}) collective-permute-start(bf16[128,4,729]{0,2,1:T(8,128)(2,1)S(1)} %slice.767), channel_id=1, source_target_pairs={{0,2},{2,0},{1,3},{3,1},{4,6},{6,4},{5,7},{7,5},{8,10},{10,8},{9,1... | collective-permute-start | bytes 2239496 | tf_op jit(solution)/shard_map/ppermute | solution.py:23
  33.7 43.7 %all-to-all-start = ((bf16[128,4,1641]{0,2,1:T(8,128)(2,1)}), bf16[128,4,1641]{0,2,1:T(8,128)(2,1)S(1)}, u32[]{:S(2)}, u32[]{:S(2)}) async-start(bf16[128,4,1641]{0,2,1:T(8,128)(2,1)} %all_to_all.50), calls=%async_computation | async-start | bytes 3375104 | tf_op jit(solution)/shard_map/all_to_all | solution.py:184
  77.4 1.2 copy-start.5
  82.3 8.9 %all-to-all-start.1 = ((bf16[4,2,1641]{2,1,0:T(2,128)(2,1)}), bf16[4,2,1641]{2,1,0:T(2,128)(2,1)S(1)}, u32[]{:S(2)}, u32[]{:S(2)}) async-start(bf16[4,2,1641]{2,1,0:T(2,128)(2,1)} %reshape.403), calls=%async_computation.1 | async-start | bytes 53248 | tf_op jit(solution)/shard_map/all_to_all | solution.py:188
  85.5 167.0 %all-reduce.34.cloned.1.call-start = ((), (), s32[]{:S(2)}) async-start(), calls=%async_computation.4 | async-start | bytes 491520 | tf_op jit(solution)/shard_map/psum | solution.py:122
  106.9 1.5 copy-start
  108.4 1.5 copy-start.1
  136.2 1.5 copy-start
  137.7 1.5 copy-start.1
  165.5 1.5 copy-start
  167.0 1.5 copy-start.1
  194.8 1.5 copy-start
  196.3 1.5 copy-start.1
  224.1 1.5 copy-start
  225.6 1.5 copy-start.1
  235.1 0.7 copy-start.4
  290.5 1.5 copy-start.2
  292.0 1.5 copy-start.3
  320.9 1.5 copy-start.2
  322.4 1.5 copy-start.3
  352.0 1.5 copy-start.2
  353.5 1.5 copy-start.3
  383.1 1.5 copy-start.2
  384.6 1.5 copy-start.3
  414.3 1.5 copy-start.2
  415.8 1.5 copy-start.3
  577.3 6.5 copy-start.6
  583.8 0.6 copy-start.9
  584.5 3.9 collective-permute-start.1
  594.1 23.7 %copy-start.7 = (f32[4,1,512]{2,0,1:T(4,128)S(1)}, f32[4,1,512]{2,0,1:T(4,128)}, u32[]{:S(2)}) copy-start(f32[4,1,512]{2,0,1:T(4,128)} %get-tuple-element.689) | copy-start | bytes 24580
  594.1 23.7 %copy-start.8 = (f32[4,1,512]{2,0,1:T(4,128)S(1)}, f32[4,1,512]{2,0,1:T(4,128)}, u32[]{:S(2)}) copy-start(f32[4,1,512]{2,0,1:T(4,128)} %get-tuple-element.691) | copy-start | bytes 24580
  612.9 10.5 %all-to-all-start.2 = ((f32[4,1,1824]{2,1,0:T(1,128)}), f32[4,1,1824]{2,1,0:T(1,128)S(1)}, u32[]{:S(2)}, u32[]{:S(2)}) async-start(f32[4,1,1824]{2,1,0:T(1,128)} %reshape.411), calls=%async_computation.2 | async-start | bytes 61440 | tf_op jit(solution)/shard_map/all_to_all | solution.py:198
Sparse Core Ops, SparseCore 0:
  236.0 16.5 all-reduce.33
where the time goes:
time: 687 us; the launch traced here: 681 us
  local copies, waits for them, and re-layouts  345 us (50%)
  other arithmetic  134 us (20%)
  waiting for transfers between devices  81 us (12%)
  blocking collectives  54.6 us (8%)
  matrix products  30.1 us (4%)
  starting transfers between devices  18.2 us (3%)
  between operations  14.6 us (2%)
    select_n x60, local copies, waits for them, and re-layouts, blocks_of(): hankels.append(jnp.where(usable, built_block, jnp.zeros_like(built_block)))  100 us
    while x200, local copies, waits for them, and re-layouts  91.7 us
    reshape x15, local copies, waits for them, and re-layouts, hankel_columns(): return level_four.reshape(LH * LH, 2 * ORDER)  59.5 us
    another operation x35, local copies, waits for them, and re-layouts, hankel_columns(): jnp.stack([level_three[..., offset:offset + LH] for offset in range(LH)], 1)  56.9 us
    select_n x30, other arithmetic, blocks_of(): hankels.append(jnp.where(usable, built_block, jnp.zeros_like(built_block)))  52.3 us
    all_to_all x1, blocking collectives, inverse_transform(): lax.all_to_all(series, 'wide', split_axis=0, concat_axis=1, tiled=True)  43.8 us
    all_to_all x1, waiting for transfers between devices, forward_transform(): lax.all_to_all(flat_rows, 'wide', split_axis=1, concat_axis=0, tiled=True)  36.9 us
    ppermute x2, waiting for transfers between devices, shifted_2(): lax.ppermute(x, axis, [(i, (i + by) % devices) for i in range(devices)])  18.9 us
  transfers between devices with their start and end apart: 6, of which 6 were waited for; matrix products, arithmetic and copies ran while one was open for 1% of the time, Pallas kernels for 0%

commit v1 on v0

v1 whole, which is shorter than its diff:
```python
import functools
import math

import jax
import jax.numpy as jnp
import numpy as np
from jax import lax
from jax.experimental import pallas as pl
from jax.experimental.pallas import tpu as pltpu
from jax.sharding import PartitionSpec as P

LH = 5
RANK = 48
FD = 1
PS = 9
TR3 = 729
INNER = LH * LH
PLANE = PS * PS
DAMP = 0.5
HIGHEST = lax.Precision.HIGHEST
LANES = 128
HALF = 64
SPAN = LH * LANES
QROWS = 32


def level_weight():
    planes = np.arange(PS)
    return np.minimum(np.minimum(planes + 1, PS - planes), LH).astype(np.float32)


def phases(time_total, freq_total):
    frequency = jnp.arange(freq_total, dtype=jnp.int32) + 1
    moments = jnp.arange(time_total, dtype=jnp.int32)
    turned = frequency[:, None] * moments[None, :] % time_total
    return turned.astype(jnp.float32) * (2.0 * math.pi / time_total)


def forward_table(time_total, freq_total):
    angles = phases(time_total, freq_total)
    factor = 1.0 / math.sqrt(time_total)
    matrix = jnp.stack([jnp.cos(angles) * factor, -jnp.sin(angles) * factor], 1)
    return matrix.reshape(2 * freq_total, time_total).astype(jnp.bfloat16)


def inverse_table(time_total, freq_total):
    angles = phases(time_total, freq_total)
    factor = 2.0 / math.sqrt(time_total)
    matrix = jnp.stack([jnp.cos(angles) * factor, -jnp.sin(angles) * factor], 1)
    return matrix.reshape(2 * freq_total, time_total)


def picker():
    table = np.zeros((SPAN, LANES), np.float32)
    for b in range(LH):
        for c in range(LH):
            for d in range(LH):
                table[b * LANES + c * PS + d, b * INNER + c * LH + d] = 1.0
    return table


def scale_table():
    w = level_weight()
    taper = w / LH
    full = taper[None, :, None, None] / (
        w[:, None, None, None] * w[None, :, None, None] * w[None, None, :, None] * w[None, None, None, :]
    )
    full = full.reshape(PS, PS, PLANE)
    both = np.concatenate([full, full], 1)
    return np.pad(both, ((0, 0), (0, 0), (0, LANES - PLANE))).astype(np.float32)


def eliminate(matrix, full):
    groups = RANK // 8
    lane = lax.broadcasted_iota(jnp.int32, (8, LANES), 1)
    sub = lax.broadcasted_iota(jnp.int32, (8, LANES), 0)
    sign = jnp.where(lax.broadcasted_iota(jnp.int32, (1, LANES), 1) < HALF, -1.0, 1.0)
    x = [matrix[8 * g : 8 * g + 8] for g in range(groups)]
    w = [jnp.where(lane == sub + 8 * g, 1.0, 0.0) for g in range(groups)]
    inverses = []
    for k in range(RANK):
        home, at = divmod(k, 8)
        row_x = x[home][at : at + 1]
        row_w = w[home][at : at + 1]
        inv = 1.0 / row_x[:, k : k + 1]
        inverses.append(inv)
        row_x = row_x * inv
        row_w = row_w * inv
        turn_x = pltpu.roll(row_x, HALF, 1) * sign
        turn_w = pltpu.roll(row_w, HALF, 1) * sign
        for g in range(groups):
            if not full and g < home:
                continue
            m_re = x[g][:, k : k + 1]
            m_im = x[g][:, HALF + k : HALF + k + 1]
            new_x = x[g] - (m_re * row_x + m_im * turn_x)
            new_w = w[g] - (m_re * row_w + m_im * turn_w)
            if g == home:
                keep = sub == at if full else sub <= at
                new_x = jnp.where(keep, x[g], new_x)
                new_w = jnp.where(keep, w[g], new_w)
            x[g] = new_x
            w[g] = new_w
    scale = []
    for g in range(groups):
        column = jnp.zeros((8, 1), jnp.float32)
        rows = lax.broadcasted_iota(jnp.int32, (8, 1), 0)
        for at in range(8):
            column = jnp.where(rows == at, inverses[8 * g + at], column)
        scale.append(column if full else jnp.sqrt(column))
    return jnp.concatenate([w[g] * scale[g] for g in range(groups)], 0)


def hermitian(left, re, im):
    gap = jnp.zeros((HALF - RANK, 2 * SPAN), jnp.float32)
    right = jnp.concatenate([re, gap, im, gap], 0)
    return lax.dot_general(
        left, right, (((1,), (1,)), ((), ())), precision=HIGHEST, preferred_element_type=jnp.float32
    )


def spread(left, top, bottom):
    gap = jnp.zeros((HALF - RANK, 2 * SPAN), jnp.float32)
    right = jnp.concatenate([top, gap, bottom, gap], 0)
    return jnp.dot(left, right, precision=HIGHEST, preferred_element_type=jnp.float32)


def frequency_kernel(x_ref, test_ref, pick_ref, pick_t_ref, scale_ref, out_ref, t_ref, y_ref, h_ref):
    rows_ea = 2 * PS
    t_ref[...] = jnp.zeros_like(t_ref)
    for q in range(INNER):
        off = q // LH * PS + q % LH
        for big in range(PS):
            piece = x_ref[big]
            if off:
                piece = pltpu.roll(piece, LANES - off, 1)
            t_ref[big, pl.ds(q, rows_ea, stride=QROWS), :] = piece
    y_ref[...] = jnp.zeros_like(y_ref)
    pick = pick_ref[...]
    part = PS * QROWS
    for e in range(2):
        for b in range(LH):
            block = jnp.concatenate(
                [t_ref[b + s, e * part : (e + 1) * part, :].astype(jnp.bfloat16) for s in range(LH)], 1
            )
            got = jnp.dot(block, pick, preferred_element_type=jnp.float32)
            for big in range(PS):
                y_ref[
                    big * LANES + b * INNER : big * LANES + (b + 1) * INNER, e * LANES : (e + 1) * LANES
                ] = got[big * QROWS : big * QROWS + INNER]
    h_ref[...] = y_ref[: PS * LANES, :].astype(jnp.bfloat16)

    def times_hankel(left):
        outs = [
            jnp.dot(left, h_ref[a * LANES : a * LANES + SPAN, :], preferred_element_type=jnp.float32)
            for a in range(LH)
        ]
        re = jnp.concatenate([o[:, :LANES] for o in outs], 1)
        im = jnp.concatenate([o[:, LANES:] for o in outs], 1)
        return re, im

    p_re, p_im = times_hankel(test_ref[...])
    straight = jnp.concatenate([p_re, p_im], 1)
    crossed = jnp.concatenate([p_im, -p_re], 1)
    gram = hermitian(straight, straight, crossed)
    root = eliminate(gram, False)
    ortho = spread(root, jnp.concatenate([p_re, -p_im], 1), jnp.concatenate([p_im, p_re], 1))
    gap = jnp.zeros((HALF - RANK, SPAN), jnp.float32)
    q_rows = jnp.concatenate([ortho[:, :SPAN], gap, ortho[:, SPAN:], gap], 0)
    q_left = q_rows.astype(jnp.bfloat16)
    mixed_re, mixed_im = times_hankel(q_left)
    c_re = mixed_re[:RANK] - mixed_im[HALF : HALF + RANK]
    c_im = mixed_im[:RANK] + mixed_re[HALF : HALF + RANK]
    coupled = jnp.concatenate([c_re, c_im], 1)
    damping = hermitian(coupled, coupled, jnp.concatenate([-c_im, c_re], 1))
    lane = lax.broadcasted_iota(jnp.int32, (RANK, LANES), 1)
    row = lax.broadcasted_iota(jnp.int32, (RANK, LANES), 0)
    diagonal = lane == row
    level = DAMP * jnp.sum(jnp.where(diagonal, damping, 0.0)) / RANK
    solved = eliminate(damping + jnp.where(diagonal, level, 0.0), True)
    coeffs = coupled - level * spread(solved, coupled, jnp.concatenate([-c_im, c_re], 1))
    f_re = coeffs[:, :SPAN].astype(jnp.bfloat16)
    f_im = coeffs[:, SPAN:].astype(jnp.bfloat16)
    gap16 = jnp.zeros((HALF - RANK, LANES), jnp.bfloat16)
    q_t = jnp.transpose(q_rows).astype(jnp.bfloat16)
    y_ref[...] = jnp.zeros_like(y_ref)
    for a in range(LH):
        at = slice(a * LANES, (a + 1) * LANES)
        left = jnp.concatenate([f_re[:, at], gap16, f_im[:, at], gap16], 0)
        right = jnp.concatenate([f_im[:, at], gap16, -f_re[:, at], gap16], 0)
        y_ref[a * LANES : a * LANES + SPAN, :] += jnp.dot(
            q_t, jnp.concatenate([left, right], 1), preferred_element_type=jnp.float32
        )
    t_ref[...] = jnp.zeros_like(t_ref)
    pick_t = pick_t_ref[...]
    for e in range(2):
        for b in range(LH):
            lines = jnp.concatenate(
                [
                    y_ref[
                        big * LANES + b * INNER : big * LANES + b * INNER + QROWS,
                        e * LANES : (e + 1) * LANES,
                    ]
                    for big in range(PS)
                ],
                0,
            )
            high = lines.astype(jnp.bfloat16)
            low = (lines - high.astype(jnp.float32)).astype(jnp.bfloat16)
            wide_lines = jnp.dot(
                jnp.concatenate([high, low], 1), pick_t, preferred_element_type=jnp.float32
            )
            for s in range(LH):
                t_ref[b + s, e * part : (e + 1) * part, :] += wide_lines[:, s * LANES : (s + 1) * LANES]
    for big in range(PS):
        total = jnp.zeros((rows_ea, LANES), jnp.float32)
        for q in range(INNER):
            off = q // LH * PS + q % LH
            piece = t_ref[big, pl.ds(q, rows_ea, stride=QROWS), :]
            total = total + (pltpu.roll(piece, off, 1) if off else piece)
        out_ref[big] = total * scale_ref[big]


def reduce_frequency(spectrum, test_rows):
    laid = jnp.transpose(spectrum, (2, 0, 1, 3)).reshape(PS, 2 * PS, PLANE)
    laid = jnp.pad(laid, ((0, 0), (0, 0), (0, LANES - PLANE)))
    pick = picker()
    pick_t = np.concatenate([pick.T, pick.T], 0)
    out = pl.pallas_call(
        frequency_kernel,
        out_shape=jax.ShapeDtypeStruct((PS, 2 * PS, LANES), jnp.float32),
        in_specs=[pl.BlockSpec(memory_space=pltpu.VMEM)] * 5,
        out_specs=pl.BlockSpec(memory_space=pltpu.VMEM),
        scratch_shapes=[
            pltpu.VMEM((PS, 2 * PS * QROWS, LANES), jnp.float32),
            pltpu.VMEM((PS * LANES + 8, 2 * LANES), jnp.float32),
            pltpu.VMEM((PS * LANES, 2 * LANES), jnp.bfloat16),
        ],
        compiler_params=pltpu.CompilerParams(vmem_limit_bytes=40 * 1024 * 1024),
    )(
        laid,
        test_rows,
        jnp.asarray(pick, jnp.bfloat16),
        jnp.asarray(pick_t, jnp.bfloat16),
        jnp.asarray(scale_table()),
    )
    return jnp.transpose(out[:, :, :PLANE].reshape(PS, 2, PS, PLANE), (1, 2, 0, 3)).reshape(2, PS, TR3)


def shift_patch(x, by):
    devices = lax.axis_size("patch")
    return lax.ppermute(x, "patch", [(i, (i + by) % devices) for i in range(devices)])


def shards(survey, test_matrix):
    wide_count = lax.axis_size("wide")
    mine = lax.axis_index("wide")
    time_local, plane_count, unused_size = survey.shape
    time_total = time_local * wide_count
    freq_total = FD * wide_count
    forward = forward_table(time_total, freq_total)
    own_forward = lax.dynamic_slice_in_dim(forward, mine * time_local, time_local, 1)
    partial = jnp.dot(
        own_forward, survey.reshape(time_local, plane_count * TR3), preferred_element_type=jnp.float32
    )
    partial = partial.reshape(wide_count, 2 * FD * plane_count * TR3)
    pieces = lax.all_to_all(partial, "wide", split_axis=0, concat_axis=0, tiled=True)
    spectra = jnp.sum(pieces, 0).astype(jnp.bfloat16).reshape(FD, 2, plane_count, TR3)
    rim = shift_patch(spectra[:, :, : LH - 1], -1)
    grid = jnp.concatenate([spectra, rim], 2).astype(jnp.float32)
    test_rows = jnp.pad(
        test_matrix.T.reshape(RANK, LH, LH * INNER), ((0, 0), (0, 0), (0, LANES - LH * INNER))
    ).reshape(RANK, SPAN)
    smooth = jnp.stack([reduce_frequency(grid[f].reshape(2, PS, PS, PLANE), test_rows) for f in range(FD)], 0)
    carried = shift_patch(smooth[:, :, LH:, :], 1)
    smooth = jnp.concatenate([smooth[:, :, : LH - 1, :] + carried, smooth[:, :, LH - 1 : LH, :]], 2)
    gathered = lax.all_gather(smooth.reshape(2 * FD, plane_count * TR3), "wide", axis=0, tiled=True)
    inverse = inverse_table(time_total, freq_total)
    own_inverse = lax.dynamic_slice_in_dim(inverse, mine * time_local, time_local, 1)
    series = lax.dot_general(
        own_inverse, gathered, (((0,), (0,)), ((), ())), precision=HIGHEST, preferred_element_type=jnp.float32
    )
    return series.reshape(time_local, plane_count, TR3)


def solution(mesh):
    return jax.shard_map(
        shards,
        mesh=mesh,
        in_specs=(P("wide", ("grp", "patch"), None), P()),
        out_specs=P("wide", ("grp", "patch"), None),
        check_vma=False,
    )
```

time: 687 us -> 64.8 us (0.09)
  local copies, waits for them, and re-layouts: 345 us -> 4.08 us
  other arithmetic: 134 us -> 0.38 us
  waiting for transfers between devices: 81 us -> 4.11 us
  blocking collectives: 54.6 us -> 25.5 us
  matrix products: 30.1 us -> 3.44 us
  Pallas kernels: 0 us -> 23.7 us
  starting transfers between devices: 18.2 us -> 3.11 us
  between operations: 14.6 us -> 0.23 us
    select_n x60 -> x0, local copies, waits for them, and re-layouts: 100 us -> none  [blocks_of(): hankels.append(jnp.where(usable, built_block, jnp.zeros_like(built_block)))]
    while x200 -> x0, local copies, waits for them, and re-layouts: 91.7 us -> none
    another operation x72 -> x1, local copies, waits for them, and re-layouts: 61.3 us -> 0.13 us  [shards(): jnp.stack([reduce_frequency(grid[f].reshape(2, PS, PS, PLANE), test_rows)...]
    reshape x20 -> x5, local copies, waits for them, and re-layouts: 63.3 us -> 3.02 us  [the longest x1 1.51 us: shards(): survey.reshape(time_local, plane_count * TR3)]
    select_n x30 -> x0, other arithmetic: 52.3 us -> none  [blocks_of(): hankels.append(jnp.where(usable, built_block, jnp.zeros_like(built_block)))]
    all_to_all x3 -> x0, waiting for transfers between devices: 47.4 us -> none  [the longest x1 36.9 us: forward_transform(): lax.all_to_all(flat_rows, 'wide', split_axis=1, concat_axis=0, tiled=True)]
    another operation x10 -> x0, other arithmetic: 34.8 us -> none  [the longest x3 9.46 us: reduce_frequency(): jnp.linalg.cholesky(shifted)]
    all_to_all x1, blocking collectives: 43.8 us -> 12 us  [shards(): lax.all_to_all(partial, 'wide', split_axis=0, concat_axis=0, tiled=True)]
  transfers between devices with their start and end apart: 6 -> 2, of which waited for: 6 -> 2; matrix products, arithmetic and copies ran while one was open for 1% -> 1% of each run, Pallas kernels for 0% -> 0%
where the time goes in v1:
time: 64.8 us; the launch traced here: 64.6 us
  blocking collectives  25.5 us (39%)
  Pallas kernels  23.7 us (37%)
  waiting for transfers between devices  4.11 us (6%)
  local copies, waits for them, and re-layouts  4.08 us (6%)
  matrix products  3.44 us (5%)
  starting transfers between devices  3.11 us (5%)
    pallas_call x1, Pallas kernels, reduce_frequency(): pl.pallas_call(frequency_kernel, out_shape=jax.ShapeDtypeStruct((PS, 2 *...  23.7 us
    all_gather x1, blocking collectives, shards(): lax.all_gather(smooth.reshape(2 * FD, plane_count * TR3), 'wide', axis=0,...  13.5 us
    all_to_all x1, blocking collectives, shards(): lax.all_to_all(partial, 'wide', split_axis=0, concat_axis=0, tiled=True)  12 us
    ppermute x2, waiting for transfers between devices, shift_patch(): lax.ppermute(x, 'patch', [(i, (i + by) % devices) for i in range(devices)])  4.11 us
    ppermute x2, starting transfers between devices, shift_patch(): lax.ppermute(x, 'patch', [(i, (i + by) % devices) for i in range(devices)])  3.11 us
    dot_general x1, matrix products, shards(): lax.dot_general(own_inverse, gathered, (((0,), (0,)), ((), ())), precisio...  3.09 us
    reshape x1, local copies, waits for them, and re-layouts, shards(): survey.reshape(time_local, plane_count * TR3)  1.51 us
    reshape x1, local copies, waits for them, and re-layouts, shards(): return series.reshape(time_local, plane_count, TR3)  1.37 us
  transfers between devices with their start and end apart: 2, of which 2 were waited for; matrix products, arithmetic and copies ran while one was open for 1% of the time, Pallas kernels for 0%

profile of v1, /device:TPU:0, one launch (start us, length us, event | category | flops | bytes accessed | tf_op | source)
XLA Modules:
  0.0 64.6 jit_solution(8407776939154134320)
XLA Ops:
  0.0 0.0 copy-start.3
  0.0 0.2 broadcast_multiply_fusion
  0.2 0.0 copy-start
  0.2 0.0 copy-start.1
  0.2 0.0 copy-start.2
  0.3 1.5 %reshape.211 = bf16[128,3645]{0,1:T(8,128)(2,1)S(1)} reshape(bf16[128,5,729]{0,2,1:T(8,128)(2,1)} %param.5) | data formatting | bytes 1866240 | tf_op jit(solution)/shard_map/reshape | solution.py:264
  1.8 0.4 fusion.7
  2.1 0.2 all_to_all.8
  2.3 12.0 %all_to_all.10 = f32[4,1,7290]{2,1,0:T(1,128)S(1)} all-to-all(f32[4,1,7290]{2,1,0:T(1,128)S(1)} %all_to_all.8), channel_id=1, replica_groups=mesh['grp'=2,'wide'=4,'patch'=2,'sub'=2] {'wide'}, dimensions={0} | all-to-all | bytes 233280 | tf_op jit(solution)/shard_map/all_to_all | solution.py:267
  14.3 0.1 reduce_sum.9
  14.5 0.1 convert_element_type.63
  14.6 1.6 %collective-permute-start = (bf16[1,2,4,729]{3,2,1,0:T(4,128)(2,1)S(1)}, bf16[1,2,4,729]{3,2,1,0:T(4,128)(2,1)S(1)}, u32[]{:S(2)}, u32[]{:S(2)}) collective-permute-start(bf16[1,2,4,729]{3,2,1,0:T(4,128)(2,1)S(1)} %slice.20), channel_id=1, source_target_pairs={{0,2},{2,0},{1,3},{3,1},{4,6},{6,4},{5,7},{7,5},{8,10},{10,8},{9,1... | collective-permute-start | bytes 35000 | tf_op jit(solution)/shard_map/ppermute | solution.py:252
  16.1 0.0 copy-done.3
  16.1 0.1 reshape.213
  16.3 0.2 convert_element_type.62
  16.5 1.8 %collective-permute-done = bf16[1,2,4,729]{3,2,1,0:T(4,128)(2,1)S(1)} collective-permute-done((bf16[1,2,4,729]{3,2,1,0:T(4,128)(2,1)S(1)}, bf16[1,2,4,729]{3,2,1,0:T(4,128)(2,1)S(1)}, u32[]{:S(2)}, u32[]{:S(2)}) %collective-permute-start) | collective-permute-done | bytes 11696 | tf_op jit(solution)/shard_map/ppermute | solution.py:252
  18.3 0.1 concatenate.11
  18.5 0.0 copy-done
  18.5 0.0 copy-done.1
  18.5 0.0 copy-done.2
  18.5 23.7 %shard_map.55 = f32[9,18,128]{2,1,0:T(8,128)S(1)} custom-call(f32[9,18,128]{2,1,0:T(8,128)S(1)} %pad_convert_fusion.x_ref, bf16[48,640]{1,0:T(8,128)(2,1)S(1)} %bitcast.19, bf16[640,128]{1,0:T(8,128)(2,1)S(1)} %copy-done.1, bf16[256,640]{1,0:T(8,128)(2,1)S(1)} %copy-done, f32[9,18,128]{2,1,0:T(8,128)S(1)} %copy-done.2), custom_call_target="tpu_custom_call" | custom-call | tf_op jit(solution)/shard_map/pallas_call | solution.py:229
  42.3 0.1 copy.21
  42.3 0.1 stack_reshape.3
  42.5 1.6 %collective-permute-start.1 = (f32[1,2,4,729]{3,1,2,0:T(2,128)S(1)}, f32[1,2,4,729]{3,1,2,0:T(2,128)S(1)}, u32[]{:S(2)}, u32[]{:S(2)}) collective-permute-start(f32[1,2,4,729]{3,1,2,0:T(2,128)S(1)} %slice.23), channel_id=1, source_target_pairs={{0,2},{2,0},{1,3},{3,1},{4,6},{6,4},{5,7},{7,5},{8,10},{10,8},{9,1... | collective-permute-start | bytes 69992 | tf_op jit(solution)/shard_map/ppermute | solution.py:252
  44.1 2.3 %collective-permute-done.1 = f32[1,2,4,729]{3,1,2,0:T(2,128)S(1)} collective-permute-done((f32[1,2,4,729]{3,1,2,0:T(2,128)S(1)}, f32[1,2,4,729]{3,1,2,0:T(2,128)S(1)}, u32[]{:S(2)}, u32[]{:S(2)}) %collective-permute-start.1) | collective-permute-done | bytes 23360 | tf_op jit(solution)/shard_map/ppermute | solution.py:252
  46.4 0.1 reshape.218
  46.5 13.5 %all-gather = f32[4,2,3645]{2,1,0:T(2,128)S(1)} all-gather(f32[1,2,3645]{2,1,0:T(2,128)S(1)} %reshape.218), channel_id=1, replica_groups=mesh['grp'=2,'wide'=4,'patch'=2,'sub'=2] {'wide'}, dimensions={0}, use_global_device_ids=true | all-gather | bytes 145800 | tf_op jit(solution)/shard_map/all_gather | solution.py:277
  60.0 0.1 reshape.219
  60.1 3.1 %fusion.4 = f32[128,3645]{0,1:T(8,128)S(1)} fusion(f32[8,3645]{1,0:T(8,128)S(1)} %reshape.219, f32[8,512]{1,0:T(8,128)S(1)} %reshape.210, s32[]{:T(128)S(6)} %select_n.39), kind=kOutput, calls=%fused_computation.17 | convolution fusion | flops 44789760 | bytes 1989124 | tf_op jit(solution)/shard_map/dot_general | solution.py:280
  63.2 1.4 %reshape.217 = f32[128,5,729]{0,2,1:T(8,128)} reshape(f32[128,3645]{0,1:T(8,128)S(1)} %fusion.4) | data formatting | bytes 3732480 | tf_op jit(solution)/shard_map/reshape | solution.py:283
  (19 shorter events, 0.2 us)
Async XLA Ops:
  0.0 16.1 %copy-start.3 = (bf16[625,48]{0,1:T(8,128)(2,1)S(1)}, bf16[625,48]{0,1:T(8,128)(2,1)}, u32[]{:S(2)}) copy-start(bf16[625,48]{0,1:T(8,128)(2,1)} %param.6) | copy-start | bytes 180004
  0.2 18.3 %copy-start = (bf16[256,640]{1,0:T(8,128)(2,1)S(1)}, bf16[256,640]{1,0:T(8,128)(2,1)}, u32[]{:S(2)}) copy-start(bf16[256,640]{1,0:T(8,128)(2,1)} %constant.47.clone.pick_t_ref) | copy-start | bytes 983044
  0.2 18.3 %copy-start.1 = (bf16[640,128]{1,0:T(8,128)(2,1)S(1)}, bf16[640,128]{1,0:T(8,128)(2,1)}, u32[]{:S(2)}) copy-start(bf16[640,128]{1,0:T(8,128)(2,1)} %constant.46.clone.pick_ref) | copy-start | bytes 491524
  0.2 18.3 %copy-start.2 = (f32[9,18,128]{2,1,0:T(8,128)S(1)}, f32[9,18,128]{2,1,0:T(8,128)}, u32[]{:S(2)}) copy-start(f32[9,18,128]{2,1,0:T(8,128)} %constant.48.clone.scale_ref) | copy-start | bytes 248836
  14.6 3.8 %collective-permute-start = (bf16[1,2,4,729]{3,2,1,0:T(4,128)(2,1)S(1)}, bf16[1,2,4,729]{3,2,1,0:T(4,128)(2,1)S(1)}, u32[]{:S(2)}, u32[]{:S(2)}) collective-permute-start(bf16[1,2,4,729]{3,2,1,0:T(4,128)(2,1)S(1)} %slice.20), channel_id=1, source_target_pairs={{0,2},{2,0},{1,3},{3,1},{4,6},{6,4},{5,7},{7,5},{8,10},{10,8},{9,1... | collective-permute-start | bytes 35000 | tf_op jit(solution)/shard_map/ppermute | solution.py:252
  42.5 3.9 %collective-permute-start.1 = (f32[1,2,4,729]{3,1,2,0:T(2,128)S(1)}, f32[1,2,4,729]{3,1,2,0:T(2,128)S(1)}, u32[]{:S(2)}, u32[]{:S(2)}) collective-permute-start(f32[1,2,4,729]{3,1,2,0:T(2,128)S(1)} %slice.23), channel_id=1, source_target_pairs={{0,2},{2,0},{1,3},{3,1},{4,6},{6,4},{5,7},{7,5},{8,10},{10,8},{9,1... | collective-permute-start | bytes 69992 | tf_op jit(solution)/shard_map/ppermute | solution.py:252

commit v2 on v1

--- a/solution.py
+++ b/solution.py
@@ -228,6 +228,7 @@
     pick_t = np.concatenate([pick.T, pick.T], 0)
     out = pl.pallas_call(
         frequency_kernel,
+        name="frequency",
         out_shape=jax.ShapeDtypeStruct((PS, 2 * PS, LANES), jnp.float32),
         in_specs=[pl.BlockSpec(memory_space=pltpu.VMEM)] * 5,
         out_specs=pl.BlockSpec(memory_space=pltpu.VMEM),
@@ -247,9 +248,100 @@
     return jnp.transpose(out[:, :, :PLANE].reshape(PS, 2, PS, PLANE), (1, 2, 0, 3)).reshape(2, PS, TR3)
 
 
-def shift_patch(x, by):
-    devices = lax.axis_size("patch")
-    return lax.ppermute(x, "patch", [(i, (i + by) % devices) for i in range(devices)])
+def exchange(by, full_ref, edge_ref, own, far, send, recv):
+    count = lax.axis_size("wide")
+    patches = lax.axis_size("patch")
+    mine = lax.axis_index("wide")
+    here = lax.axis_index("patch")
+    target_patch = lax.rem(here + by + patches, patches)
+    source_patch = lax.rem(here - by + patches, patches)
+    barrier = pltpu.get_barrier_semaphore()
+    for k in range(count):
+        other = lax.rem(mine + k, count)
+        if k:
+            pl.semaphore_signal(barrier, inc=1, device_id={"wide": other}, device_id_type=pl.DeviceIdType.MESH)
+        pl.semaphore_signal(
+            barrier,
+            inc=1,
+            device_id={"wide": other, "patch": source_patch},
+            device_id_type=pl.DeviceIdType.MESH,
+        )
+    pl.semaphore_wait(barrier, 2 * count - 1)
+
+    def block(ref, index):
+        return ref.at[0] if ref.shape[0] == 1 else ref.at[index]
+
+    def full_copy(target, slot):
+        return pltpu.make_async_remote_copy(
+            src_ref=block(full_ref, target),
+            dst_ref=own.at[slot],
+            send_sem=send.at[0, target],
+            recv_sem=recv.at[0, slot],
+            device_id={"wide": target},
+            device_id_type=pl.DeviceIdType.MESH,
+        )
+
+    def edge_copy(target, slot):
+        return pltpu.make_async_remote_copy(
+            src_ref=block(edge_ref, target),
+            dst_ref=far.at[slot],
+            send_sem=send.at[1, target],
+            recv_sem=recv.at[1, slot],
+            device_id={"wide": target, "patch": target_patch},
+            device_id_type=pl.DeviceIdType.MESH,
+        )
+
+    order = list(range(count - 1, -1, -1))
+    for k in order:
+        target = lax.rem(mine + k, count)
+        if k:
+            full_copy(target, mine).start()
+        edge_copy(target, mine).start()
+    own[mine] = block(full_ref, mine)[...]
+    for k in order:
+        source = lax.rem(mine + count - k, count)
+        if k:
+            full_copy(source, source).wait_recv()
+        edge_copy(source, source).wait_recv()
+    for k in order:
+        target = lax.rem(mine + k, count)
+        if k:
+            full_copy(target, mine).wait_send()
+        edge_copy(target, mine).wait_send()
+
+
+def collect_kernel(full_ref, edge_ref, own_out, far_out, own, far, send, recv):
+    exchange(-1, full_ref, edge_ref, own, far, send, recv)
+    own_out[...] = jnp.sum(own[...], 0).astype(jnp.bfloat16).astype(jnp.float32)
+    far_out[...] = jnp.sum(far[...], 0).astype(jnp.bfloat16).astype(jnp.float32)
+
+
+def share_kernel(full_ref, edge_ref, out_ref, own, far, send, recv):
+    exchange(1, full_ref, edge_ref, own, far, send, recv)
+    width = far.shape[-1]
+    out_ref[...] = own[...]
+    out_ref[:, :, :width] = own[:, :, :width] + far[...]
+
+
+def exchange_call(kernel, name, full, edge, outs, identity):
+    count = lax.axis_size("wide")
+    shapes = [(count,) + full.shape[1:], (count,) + edge.shape[1:]]
+    return pl.pallas_call(
+        kernel,
+        name=name,
+        out_shape=[jax.ShapeDtypeStruct(o, jnp.float32) for o in outs],
+        in_specs=[pl.BlockSpec(memory_space=pltpu.VMEM)] * 2,
+        out_specs=[pl.BlockSpec(memory_space=pltpu.VMEM)] * len(outs),
+        scratch_shapes=[
+            pltpu.VMEM(shapes[0], jnp.float32),
+            pltpu.VMEM(shapes[1], jnp.float32),
+            pltpu.SemaphoreType.DMA((2, count)),
+            pltpu.SemaphoreType.DMA((2, count)),
+        ],
+        compiler_params=pltpu.CompilerParams(
+            collective_id=identity, has_side_effects=True, vmem_limit_bytes=40 * 1024 * 1024
+        ),
+    )(full, edge)
 
 
 def shards(survey, test_matrix):
@@ -258,27 +350,37 @@
     time_local, plane_count, unused_size = survey.shape
     time_total = time_local * wide_count
     freq_total = FD * wide_count
+    traces = plane_count * TR3
+    margin = (LH - 1) * TR3
     forward = forward_table(time_total, freq_total)
     own_forward = lax.dynamic_slice_in_dim(forward, mine * time_local, time_local, 1)
-    partial = jnp.dot(
-        own_forward, survey.reshape(time_local, plane_count * TR3), preferred_element_type=jnp.float32
-    )
-    partial = partial.reshape(wide_count, 2 * FD * plane_count * TR3)
-    pieces = lax.all_to_all(partial, "wide", split_axis=0, concat_axis=0, tiled=True)
-    spectra = jnp.sum(pieces, 0).astype(jnp.bfloat16).reshape(FD, 2, plane_count, TR3)
-    rim = shift_patch(spectra[:, :, : LH - 1], -1)
-    grid = jnp.concatenate([spectra, rim], 2).astype(jnp.float32)
+    partial = jnp.dot(own_forward, survey.reshape(time_local, traces), preferred_element_type=jnp.float32)
+    partial = partial.reshape(wide_count, 2 * FD, traces)
+    spectra, rim = exchange_call(
+        collect_kernel, "collect", partial, partial[:, :, :margin], [(2 * FD, traces), (2 * FD, margin)], 0
+    )
+    grid = jnp.concatenate([spectra, rim], 1).reshape(FD, 2, PS, PS, PLANE)
     test_rows = jnp.pad(
         test_matrix.T.reshape(RANK, LH, LH * INNER), ((0, 0), (0, 0), (0, LANES - LH * INNER))
     ).reshape(RANK, SPAN)
-    smooth = jnp.stack([reduce_frequency(grid[f].reshape(2, PS, PS, PLANE), test_rows) for f in range(FD)], 0)
-    carried = shift_patch(smooth[:, :, LH:, :], 1)
-    smooth = jnp.concatenate([smooth[:, :, : LH - 1, :] + carried, smooth[:, :, LH - 1 : LH, :]], 2)
-    gathered = lax.all_gather(smooth.reshape(2 * FD, plane_count * TR3), "wide", axis=0, tiled=True)
+    smooth = jnp.stack([reduce_frequency(grid[f], test_rows) for f in range(FD)], 0)
+    smooth = smooth.reshape(1, 2 * FD, PS * TR3)
+    (gathered,) = exchange_call(
+        share_kernel,
+        "share",
+        smooth[:, :, :traces],
+        smooth[:, :, traces:],
+        [(wide_count, 2 * FD, traces)],
+        1,
+    )
     inverse = inverse_table(time_total, freq_total)
     own_inverse = lax.dynamic_slice_in_dim(inverse, mine * time_local, time_local, 1)
     series = lax.dot_general(
-        own_inverse, gathered, (((0,), (0,)), ((), ())), precision=HIGHEST, preferred_element_type=jnp.float32
+        own_inverse,
+        gathered.reshape(2 * freq_total, traces),
+        (((0,), (0,)), ((), ())),
+        precision=HIGHEST,
+        preferred_element_type=jnp.float32,
     )
     return series.reshape(time_local, plane_count, TR3)
 

time: 64.8 us -> 53.3 us (0.82)
  blocking collectives: 25.5 us -> 0 us
  Pallas kernels: 23.7 us -> 44.3 us
  waiting for transfers between devices: 4.11 us -> 0 us
  starting transfers between devices: 3.11 us -> 0 us
  matrix products: 3.44 us -> 4.74 us
    pallas_call x1 -> x3, Pallas kernels: 23.7 us -> 44.3 us  [the longest x1 23.7 us: reduce_frequency(): pl.pallas_call(frequency_kernel, name='frequency', out_shape=jax.ShapeDty...]
    all_gather x1 -> x0, blocking collectives: 13.5 us -> none  [shards(): lax.all_gather(smooth.reshape(2 * FD, plane_count * TR3), 'wide', axis=0,...]
    all_to_all x1 -> x0, blocking collectives: 12 us -> none  [shards(): lax.all_to_all(partial, 'wide', split_axis=0, concat_axis=0, tiled=True)]
    ppermute x2 -> x0, waiting for transfers between devices: 4.11 us -> none  [shift_patch(): lax.ppermute(x, 'patch', [(i, (i + by) % devices) for i in range(devices)])]
    ppermute x2 -> x0, starting transfers between devices: 3.11 us -> none  [shift_patch(): lax.ppermute(x, 'patch', [(i, (i + by) % devices) for i in range(devices)])]
    dot_general x2, matrix products: 3.44 us -> 4.74 us  [the longest x1 4.39 us: shards(): lax.dot_general(own_inverse, gathered.reshape(2 * freq_total, traces), ((...]
    reshape x2, local copies, waits for them, and re-layouts: 2.87 us -> 1.59 us  [the longest x1 1.51 us: shards(): survey.reshape(time_local, traces)]
    reshape x1, local copies, waits for them, and re-layouts: 0.12 us -> 0.95 us  [shards(): test_matrix.T.reshape(RANK, LH, LH * INNER)]
  transfers between devices with their start and end apart: 2 -> 0, of which waited for: 2 -> 0; matrix products, arithmetic and copies ran while one was open for 1% -> 0% of each run, Pallas kernels for 0% -> 0%
where the time goes in v2:
time: 53.3 us; the launch traced here: 53.1 us
  Pallas kernels  44.3 us (83%)
  matrix products  4.74 us (9%)
  local copies, waits for them, and re-layouts  3.51 us (7%)
    pallas_call x1, Pallas kernels, reduce_frequency(): pl.pallas_call(frequency_kernel, name='frequency', out_shape=jax.ShapeDty...  23.7 us
    pallas_call x2, Pallas kernels, exchange_call(): pl.pallas_call(kernel, name=name, out_shape=[jax.ShapeDtypeStruct(o, jnp....  20.6 us
    dot_general x1, matrix products, shards(): lax.dot_general(own_inverse, gathered.reshape(2 * freq_total, traces), ((...  4.39 us
    reshape x1, local copies, waits for them, and re-layouts, shards(): survey.reshape(time_local, traces)  1.51 us

profile of v2, /device:TPU:0, one launch (start us, length us, event | category | flops | bytes accessed | tf_op | source)
XLA Modules:
  0.0 53.1 jit_solution(483909746098666577)
XLA Ops:
  0.0 0.2 broadcast_multiply_fusion
  0.3 1.0 %reshape.184 = bf16[48,5,125]{2,1,0:T(8,128)(2,1)S(1)} reshape(bf16[48,625]{1,0:T(8,128)(2,1)} %bitcast.27) | data formatting | bytes 120000 | tf_op jit(solution)/shard_map/reshape | solution.py:364
  1.3 0.0 copy-start
  1.3 0.0 copy-start.1
  1.3 0.0 copy-start.2
  1.3 1.5 %reshape.188 = bf16[128,3645,1]{0,1,2:T(8,128)(2,1)S(1)} reshape(bf16[128,5,729]{0,2,1:T(8,128)(2,1)} %param.5) | data formatting | bytes 1866240 | tf_op jit(solution)/shard_map/reshape | solution.py:357
  2.8 0.4 fusion.10.full_ref
  3.2 11.9 %collect.1 = (f32[2,3645]{1,0:T(2,128)S(1)}, f32[2,2916]{1,0:T(2,128)S(1)}) custom-call(f32[4,2,3645]{2,1,0:T(2,128)S(1)} %fusion.10.full_ref, f32[4,2,2916]{2,1,0:T(2,128)S(1)} %slice.16.edge_ref), custom_call_target="tpu_custom_call" | custom-call | tf_op jit(solution)/shard_map/collect/pallas_call | solution.py:329
  15.1 0.1 pad_maximum_fusion
  15.2 0.2 squeeze_reshape.3
  15.4 0.0 copy-done
  15.4 0.0 copy-done.1
  15.4 0.0 copy-done.2
  15.5 23.7 %frequency.1 = f32[9,18,128]{2,1,0:T(8,128)S(1)} custom-call(f32[9,18,128]{2,1,0:T(8,128)S(1)} %pad.8.x_ref, bf16[48,640]{1,0:T(8,128)(2,1)S(1)} %bitcast.22, bf16[640,128]{1,0:T(8,128)(2,1)S(1)} %copy-done.1, bf16[256,640]{1,0:T(8,128)(2,1)S(1)} %copy-done, f32[9,18,128]{2,1,0:T(8,128)S(1)} %copy-done.2), custom_call_target="tpu_custom_call" | custom-call | tf_op jit(solution)/shard_map/frequency/pallas_call | solution.py:229
  39.2 0.1 copy.28
  39.2 0.2 reshape_stack_reshape.3
  39.4 0.1 slice.19.edge_ref
  39.5 8.8 %share.1 = f32[4,2,3645]{2,1,0:T(2,128)S(1)} custom-call(f32[1,2,3645]{2,1,0:T(2,128)S(1)} %slice.18.full_ref, f32[1,2,2916]{2,1,0:T(2,128)S(1)} %slice.19.edge_ref), custom_call_target="tpu_custom_call" | custom-call | tf_op jit(solution)/shard_map/share/pallas_call | solution.py:329
  48.3 0.1 reshape.187
  48.4 0.3 dot_general.15
  48.7 4.4 %fusion = f32[128,5,729]{0,2,1:T(8,128)} fusion(f32[5,729,8]{1,0,2:T(8,128)S(1)} %dot_general.15, f32[8,512]{1,0:T(8,128)S(1)} %reshape.181, s32[]{:T(128)S(6)} %select_n.39), kind=kOutput, calls=%fused_computation | convolution fusion | flops 44789760 | bytes 2066948 | tf_op jit(solution)/shard_map/dot_general | solution.py:378
  (15 shorter events, 0.2 us)
Async XLA Ops:
  1.3 14.1 %copy-start = (bf16[256,640]{1,0:T(8,128)(2,1)S(1)}, bf16[256,640]{1,0:T(8,128)(2,1)}, u32[]{:S(2)}) copy-start(bf16[256,640]{1,0:T(8,128)(2,1)} %constant.45.clone.pick_t_ref) | copy-start | bytes 983044
  1.3 14.1 %copy-start.1 = (bf16[640,128]{1,0:T(8,128)(2,1)S(1)}, bf16[640,128]{1,0:T(8,128)(2,1)}, u32[]{:S(2)}) copy-start(bf16[640,128]{1,0:T(8,128)(2,1)} %constant.44.clone.pick_ref) | copy-start | bytes 491524
  1.3 14.1 %copy-start.2 = (f32[9,18,128]{2,1,0:T(8,128)S(1)}, f32[9,18,128]{2,1,0:T(8,128)}, u32[]{:S(2)}) copy-start(f32[9,18,128]{2,1,0:T(8,128)} %constant.46.clone.scale_ref) | copy-start | bytes 248836

commit v3 on v2

--- a/solution.py
+++ b/solution.py
@@ -82,19 +82,22 @@
         home, at = divmod(k, 8)
         row_x = x[home][at : at + 1]
         row_w = w[home][at : at + 1]
-        inv = 1.0 / row_x[:, k : k + 1]
+        first = 0 if full else home
+        m_re = {g: jnp.broadcast_to(x[g][:, k : k + 1], (8, LANES)) for g in range(first, groups)}
+        m_im = {
+            g: jnp.broadcast_to(x[g][:, HALF + k : HALF + k + 1], (8, LANES)) for g in range(first, groups)
+        }
+        turn_x = pltpu.roll(row_x, HALF, 1) * sign
+        turn_w = pltpu.roll(row_w, HALF, 1) * sign
+        inv = 1.0 / m_re[home][at : at + 1]
         inverses.append(inv)
         row_x = row_x * inv
         row_w = row_w * inv
-        turn_x = pltpu.roll(row_x, HALF, 1) * sign
-        turn_w = pltpu.roll(row_w, HALF, 1) * sign
-        for g in range(groups):
-            if not full and g < home:
-                continue
-            m_re = x[g][:, k : k + 1]
-            m_im = x[g][:, HALF + k : HALF + k + 1]
-            new_x = x[g] - (m_re * row_x + m_im * turn_x)
-            new_w = w[g] - (m_re * row_w + m_im * turn_w)
+        turn_x = turn_x * inv
+        turn_w = turn_w * inv
+        for g in range(first, groups):
+            new_x = x[g] - (m_re[g] * row_x + m_im[g] * turn_x)
+            new_w = w[g] - (m_re[g] * row_w + m_im[g] * turn_w)
             if g == home:
                 keep = sub == at if full else sub <= at
                 new_x = jnp.where(keep, x[g], new_x)
@@ -103,10 +106,9 @@
             w[g] = new_w
     scale = []
     for g in range(groups):
-        column = jnp.zeros((8, 1), jnp.float32)
-        rows = lax.broadcasted_iota(jnp.int32, (8, 1), 0)
+        column = jnp.zeros((8, LANES), jnp.float32)
         for at in range(8):
-            column = jnp.where(rows == at, inverses[8 * g + at], column)
+            column = jnp.where(sub == at, inverses[8 * g + at], column)
         scale.append(column if full else jnp.sqrt(column))
     return jnp.concatenate([w[g] * scale[g] for g in range(groups)], 0)
 
@@ -248,28 +250,28 @@
     return jnp.transpose(out[:, :, :PLANE].reshape(PS, 2, PS, PLANE), (1, 2, 0, 3)).reshape(2, PS, TR3)
 
 
-def exchange(by, full_ref, edge_ref, own, far, send, recv):
+def exchange(by, full_ref, edge_ref, own, far, send, recv, consume):
     count = lax.axis_size("wide")
     patches = lax.axis_size("patch")
     mine = lax.axis_index("wide")
     here = lax.axis_index("patch")
+    core = lax.axis_index("sub")
     target_patch = lax.rem(here + by + patches, patches)
     source_patch = lax.rem(here - by + patches, patches)
     barrier = pltpu.get_barrier_semaphore()
+    mesh_ids = pl.DeviceIdType.MESH
+    pl.semaphore_signal(barrier, inc=1, device_id={"sub": 1 - core}, device_id_type=mesh_ids)
     for k in range(count):
         other = lax.rem(mine + k, count)
         if k:
-            pl.semaphore_signal(barrier, inc=1, device_id={"wide": other}, device_id_type=pl.DeviceIdType.MESH)
+            pl.semaphore_signal(barrier, inc=1, device_id={"wide": other}, device_id_type=mesh_ids)
         pl.semaphore_signal(
-            barrier,
-            inc=1,
-            device_id={"wide": other, "patch": source_patch},
-            device_id_type=pl.DeviceIdType.MESH,
+            barrier, inc=1, device_id={"wide": other, "patch": source_patch}, device_id_type=mesh_ids
         )
-    pl.semaphore_wait(barrier, 2 * count - 1)
+    pl.semaphore_wait(barrier, 2 * count)
 
     def block(ref, index):
-        return ref.at[0] if ref.shape[0] == 1 else ref.at[index]
+        return ref.at[core] if ref.shape[0] == 2 else ref.at[2 * index + core]
 
     def full_copy(target, slot):
         return pltpu.make_async_remote_copy(
@@ -278,7 +280,7 @@
             send_sem=send.at[0, target],
             recv_sem=recv.at[0, slot],
             device_id={"wide": target},
-            device_id_type=pl.DeviceIdType.MESH,
+            device_id_type=mesh_ids,
         )
 
     def edge_copy(target, slot):
@@ -288,7 +290,7 @@
             send_sem=send.at[1, target],
             recv_sem=recv.at[1, slot],
             device_id={"wide": target, "patch": target_patch},
-            device_id_type=pl.DeviceIdType.MESH,
+            device_id_type=mesh_ids,
         )
 
     order = list(range(count - 1, -1, -1))
@@ -298,11 +300,12 @@
             full_copy(target, mine).start()
         edge_copy(target, mine).start()
     own[mine] = block(full_ref, mine)[...]
-    for k in order:
+    for k in order[::-1]:
         source = lax.rem(mine + count - k, count)
         if k:
             full_copy(source, source).wait_recv()
         edge_copy(source, source).wait_recv()
+        consume(source)
     for k in order:
         target = lax.rem(mine + k, count)
         if k:
@@ -310,22 +313,59 @@
         edge_copy(target, mine).wait_send()
 
 
-def collect_kernel(full_ref, edge_ref, own_out, far_out, own, far, send, recv):
-    exchange(-1, full_ref, edge_ref, own, far, send, recv)
-    own_out[...] = jnp.sum(own[...], 0).astype(jnp.bfloat16).astype(jnp.float32)
-    far_out[...] = jnp.sum(far[...], 0).astype(jnp.bfloat16).astype(jnp.float32)
-
-
-def share_kernel(full_ref, edge_ref, out_ref, own, far, send, recv):
-    exchange(1, full_ref, edge_ref, own, far, send, recv)
+def to_mate(source, target, send_sem, recv_sem):
+    return pltpu.make_async_remote_copy(
+        src_ref=source,
+        dst_ref=target,
+        send_sem=send_sem,
+        recv_sem=recv_sem,
+        device_id={"sub": 1 - lax.axis_index("sub")},
+        device_id_type=pl.DeviceIdType.MESH,
+    )
+
+
+def collect_kernel(full_ref, edge_ref, own_out, far_out, own, far, send, recv, stage, mate, mate_send, mate_recv):
+    core = lax.axis_index("sub")
+    margin = far.shape[-1]
+    traces = own.shape[-1]
+    exchange(-1, full_ref, edge_ref, own, far, send, recv, lambda source: None)
+    stage[0, :, :traces] = jnp.sum(own[...], 0).astype(jnp.bfloat16).astype(jnp.float32)
+    stage[1] = jnp.zeros_like(stage[1])
+    stage[1, :, :margin] = jnp.sum(far[...], 0).astype(jnp.bfloat16).astype(jnp.float32)
+    copies = [to_mate(stage.at[i], mate.at[i], mate_send.at[i], mate_recv.at[i]) for i in range(2)]
+    for copy in copies:
+        copy.start()
+    own_out[pl.ds(core, 1), :] = stage[0, :, :traces]
+    far_out[pl.ds(core, 1), :] = stage[1, :, :margin]
+    for copy in copies:
+        copy.wait()
+    own_out[pl.ds(1 - core, 1), :] = mate[0, :, :traces]
+    far_out[pl.ds(1 - core, 1), :] = mate[1, :, :margin]
+
+
+def share_kernel(full_ref, edge_ref, out_ref, own, far, send, recv, stage, mate, mate_send, mate_recv):
+    core = lax.axis_index("sub")
+    count = lax.axis_size("wide")
     width = far.shape[-1]
-    out_ref[...] = own[...]
-    out_ref[:, :, :width] = own[:, :, :width] + far[...]
-
-
-def exchange_call(kernel, name, full, edge, outs, identity):
+
+    def mate_copy(slot):
+        return to_mate(stage.at[slot], mate.at[slot], mate_send.at[slot], mate_recv.at[slot])
+
+    def consume(slot):
+        stage[slot] = own[slot]
+        stage[slot, :, :width] = own[slot, :, :width] + far[slot]
+        mate_copy(slot).start()
+        out_ref[pl.ds(2 * slot + core, 1), :] = stage[slot]
+
+    exchange(1, full_ref, edge_ref, own, far, send, recv, consume)
+    for slot in range(count):
+        mate_copy(slot).wait()
+        out_ref[pl.ds(2 * slot + 1 - core, 1), :] = mate[slot]
+
+
+def exchange_call(kernel, name, full, edge, outs, slots, identity):
     count = lax.axis_size("wide")
-    shapes = [(count,) + full.shape[1:], (count,) + edge.shape[1:]]
+    traces = full.shape[-1]
     return pl.pallas_call(
         kernel,
         name=name,
@@ -333,10 +373,14 @@
         in_specs=[pl.BlockSpec(memory_space=pltpu.VMEM)] * 2,
         out_specs=[pl.BlockSpec(memory_space=pltpu.VMEM)] * len(outs),
         scratch_shapes=[
-            pltpu.VMEM(shapes[0], jnp.float32),
-            pltpu.VMEM(shapes[1], jnp.float32),
+            pltpu.VMEM((count, 1, traces), jnp.float32),
+            pltpu.VMEM((count, 1, edge.shape[-1]), jnp.float32),
             pltpu.SemaphoreType.DMA((2, count)),
             pltpu.SemaphoreType.DMA((2, count)),
+            pltpu.VMEM((slots, 1, traces), jnp.float32),
+            pltpu.VMEM((slots, 1, traces), jnp.float32),
+            pltpu.SemaphoreType.DMA((slots,)),
+            pltpu.SemaphoreType.DMA((slots,)),
         ],
         compiler_params=pltpu.CompilerParams(
             collective_id=identity, has_side_effects=True, vmem_limit_bytes=40 * 1024 * 1024
@@ -355,29 +399,30 @@
     forward = forward_table(time_total, freq_total)
     own_forward = lax.dynamic_slice_in_dim(forward, mine * time_local, time_local, 1)
     partial = jnp.dot(own_forward, survey.reshape(time_local, traces), preferred_element_type=jnp.float32)
-    partial = partial.reshape(wide_count, 2 * FD, traces)
+    partial = partial.reshape(2 * freq_total, 1, traces)
     spectra, rim = exchange_call(
-        collect_kernel, "collect", partial, partial[:, :, :margin], [(2 * FD, traces), (2 * FD, margin)], 0
+        collect_kernel, "collect", partial, partial[:, :, :margin], [(2 * FD, traces), (2 * FD, margin)], 2, 0
     )
     grid = jnp.concatenate([spectra, rim], 1).reshape(FD, 2, PS, PS, PLANE)
     test_rows = jnp.pad(
         test_matrix.T.reshape(RANK, LH, LH * INNER), ((0, 0), (0, 0), (0, LANES - LH * INNER))
     ).reshape(RANK, SPAN)
     smooth = jnp.stack([reduce_frequency(grid[f], test_rows) for f in range(FD)], 0)
-    smooth = smooth.reshape(1, 2 * FD, PS * TR3)
+    smooth = smooth.reshape(2 * FD, 1, PS * TR3)
     (gathered,) = exchange_call(
         share_kernel,
         "share",
         smooth[:, :, :traces],
         smooth[:, :, traces:],
-        [(wide_count, 2 * FD, traces)],
+        [(2 * freq_total, traces)],
+        wide_count,
         1,
     )
     inverse = inverse_table(time_total, freq_total)
     own_inverse = lax.dynamic_slice_in_dim(inverse, mine * time_local, time_local, 1)
     series = lax.dot_general(
         own_inverse,
-        gathered.reshape(2 * freq_total, traces),
+        gathered,
         (((0,), (0,)), ((), ())),
         precision=HIGHEST,
         preferred_element_type=jnp.float32,

time: 53.3 us -> 45.4 us (0.85)
  Pallas kernels: 44.3 us -> 36.5 us
  matrix products: 4.74 us -> 3.61 us
  local copies, waits for them, and re-layouts: 3.51 us -> 4.62 us
    pallas_call x1, Pallas kernels: 23.7 us -> 17.3 us  [reduce_frequency(): pl.pallas_call(frequency_kernel, name='frequency', out_shape=jax.ShapeDty...]
    pallas_call x2, Pallas kernels: 20.6 us -> 19.1 us  [exchange_call(): pl.pallas_call(kernel, name=name, out_shape=[jax.ShapeDtypeStruct(o, jnp....]
    reshape x1 -> x2, local copies, waits for them, and re-layouts: 0.08 us -> 1.46 us  [the longest x1 1.37 us: shards(): return series.reshape(time_local, plane_count, TR3)]
    dot_general x1, matrix products: 4.39 us -> 3.26 us  [shards(): lax.dot_general(own_inverse, gathered, (((0,), (0,)), ((), ())), precisio...]
where the time goes in v3:
time: 45.4 us; the launch traced here: 45.2 us
  Pallas kernels  36.5 us (80%)
  local copies, waits for them, and re-layouts  4.62 us (10%)
  matrix products  3.61 us (8%)
    pallas_call x2, Pallas kernels, exchange_call(): pl.pallas_call(kernel, name=name, out_shape=[jax.ShapeDtypeStruct(o, jnp....  19.1 us
    pallas_call x1, Pallas kernels, reduce_frequency(): pl.pallas_call(frequency_kernel, name='frequency', out_shape=jax.ShapeDty...  17.3 us
    dot_general x1, matrix products, shards(): lax.dot_general(own_inverse, gathered, (((0,), (0,)), ((), ())), precisio...  3.26 us
    reshape x1, local copies, waits for them, and re-layouts, shards(): survey.reshape(time_local, traces)  1.51 us
    reshape x1, local copies, waits for them, and re-layouts, shards(): return series.reshape(time_local, plane_count, TR3)  1.37 us
    reshape x1, local copies, waits for them, and re-layouts, shards(): test_matrix.T.reshape(RANK, LH, LH * INNER)  0.95 us

profile of v3, /device:TPU:0, one launch (start us, length us, event | category | flops | bytes accessed | tf_op | source)
XLA Modules:
  0.0 45.2 jit_solution(3939793316562139292)
XLA Ops:
  0.0 0.2 broadcast_multiply_fusion
  0.3 1.0 %reshape.184 = bf16[48,5,125]{2,1,0:T(8,128)(2,1)S(1)} reshape(bf16[48,625]{1,0:T(8,128)(2,1)} %bitcast.21) | data formatting | bytes 120000 | tf_op jit(solution)/shard_map/reshape | solution.py:408
  1.3 0.0 copy-start
  1.3 0.0 copy-start.1
  1.3 0.0 copy-start.2
  1.3 1.5 %reshape.181 = bf16[128,3645]{0,1:T(8,128)(2,1)S(1)} reshape(bf16[128,5,729]{0,2,1:T(8,128)(2,1)} %param.5) | data formatting | bytes 1866240 | tf_op jit(solution)/shard_map/reshape | solution.py:401
  2.8 0.4 fusion.7
  3.2 0.1 reshape.182.full_ref
  3.3 10.6 %collect.1 = (f32[2,3645]{1,0:T(2,128)S(1)}, f32[2,2916]{1,0:T(2,128)S(1)}) custom-call(f32[8,1,3645]{2,1,0:T(1,128)S(1)} %reshape.182.full_ref, f32[8,1,2916]{2,1,0:T(1,128)S(1)} %slice.16.edge_ref), custom_call_target="tpu_custom_call" | custom-call | tf_op jit(solution)/shard_map/collect/pallas_call | solution.py:369
  13.9 0.1 pad_maximum_fusion
  14.0 0.2 squeeze_reshape.3
  14.2 0.0 copy-done
  14.2 0.0 copy-done.1
  14.2 0.0 copy-done.2
  14.2 17.3 %frequency.1 = f32[9,18,128]{2,1,0:T(8,128)S(1)} custom-call(f32[9,18,128]{2,1,0:T(8,128)S(1)} %pad.8.x_ref, bf16[48,640]{1,0:T(8,128)(2,1)S(1)} %bitcast.17, bf16[640,128]{1,0:T(8,128)(2,1)S(1)} %copy-done.1, bf16[256,640]{1,0:T(8,128)(2,1)S(1)} %copy-done, f32[9,18,128]{2,1,0:T(8,128)S(1)} %copy-done.2), custom_call_target="tpu_custom_call" | custom-call | tf_op jit(solution)/shard_map/frequency/pallas_call | solution.py:231
  31.6 0.1 copy.19
  31.6 0.2 reshape_stack_reshape.4
  31.8 0.1 slice.19.edge_ref
  32.0 8.6 %share.1 = f32[8,3645]{1,0:T(8,128)S(1)} custom-call(f32[2,1,3645]{2,1,0:T(1,128)S(1)} %slice.18.full_ref, f32[2,1,2916]{2,1,0:T(1,128)S(1)} %slice.19.edge_ref), custom_call_target="tpu_custom_call" | custom-call | tf_op jit(solution)/shard_map/share/pallas_call | solution.py:369
  40.5 3.3 %fusion.4 = f32[128,3645]{0,1:T(8,128)S(1)} fusion(f32[8,3645]{1,0:T(8,128)S(1)} %share.1, f32[8,512]{1,0:T(8,128)S(1)} %reshape.180, s32[]{:T(128)S(6)} %select_n.39), kind=kOutput, calls=%fused_computation.14 | convolution fusion | flops 44789760 | bytes 1989124 | tf_op jit(solution)/shard_map/dot_general | solution.py:423
  43.8 1.4 %reshape.187 = f32[128,5,729]{0,2,1:T(8,128)} reshape(f32[128,3645]{0,1:T(8,128)S(1)} %fusion.4) | data formatting | bytes 3732480 | tf_op jit(solution)/shard_map/reshape | solution.py:430
  (14 shorter events, 0.2 us)
Async XLA Ops:
  1.3 12.9 %copy-start = (bf16[256,640]{1,0:T(8,128)(2,1)S(1)}, bf16[256,640]{1,0:T(8,128)(2,1)}, u32[]{:S(2)}) copy-start(bf16[256,640]{1,0:T(8,128)(2,1)} %constant.45.clone.pick_t_ref) | copy-start | bytes 983044
  1.3 12.9 %copy-start.1 = (bf16[640,128]{1,0:T(8,128)(2,1)S(1)}, bf16[640,128]{1,0:T(8,128)(2,1)}, u32[]{:S(2)}) copy-start(bf16[640,128]{1,0:T(8,128)(2,1)} %constant.44.clone.pick_ref) | copy-start | bytes 491524
  1.3 12.9 %copy-start.2 = (f32[9,18,128]{2,1,0:T(8,128)S(1)}, f32[9,18,128]{2,1,0:T(8,128)}, u32[]{:S(2)}) copy-start(f32[9,18,128]{2,1,0:T(8,128)} %constant.46.clone.scale_ref) | copy-start | bytes 248836

commit v4 on v3

--- a/solution.py
+++ b/solution.py
@@ -29,25 +29,15 @@
     return np.minimum(np.minimum(planes + 1, PS - planes), LH).astype(np.float32)
 
 
-def phases(time_total, freq_total):
-    frequency = jnp.arange(freq_total, dtype=jnp.int32) + 1
-    moments = jnp.arange(time_total, dtype=jnp.int32)
-    turned = frequency[:, None] * moments[None, :] % time_total
-    return turned.astype(jnp.float32) * (2.0 * math.pi / time_total)
-
-
-def forward_table(time_total, freq_total):
-    angles = phases(time_total, freq_total)
-    factor = 1.0 / math.sqrt(time_total)
-    matrix = jnp.stack([jnp.cos(angles) * factor, -jnp.sin(angles) * factor], 1)
-    return matrix.reshape(2 * freq_total, time_total).astype(jnp.bfloat16)
-
-
-def inverse_table(time_total, freq_total):
-    angles = phases(time_total, freq_total)
-    factor = 2.0 / math.sqrt(time_total)
-    matrix = jnp.stack([jnp.cos(angles) * factor, -jnp.sin(angles) * factor], 1)
-    return matrix.reshape(2 * freq_total, time_total)
+def tables(time_total, freq_total):
+    turned = np.outer(np.arange(freq_total) + 1, np.arange(time_total)) % time_total
+    angles = turned * (2.0 * math.pi / time_total)
+    waves = np.stack([np.cos(angles), -np.sin(angles)], 1).reshape(2 * freq_total, time_total)
+    forward = (waves / math.sqrt(time_total)).astype(np.float32)
+    inverse = (waves * (2.0 / math.sqrt(time_total))).astype(np.float32)
+    high = inverse.astype(jnp.bfloat16)
+    low = (inverse - high.astype(np.float32)).astype(jnp.bfloat16)
+    return forward.astype(jnp.bfloat16), np.concatenate([high, low, high], 0)
 
 
 def picker():
@@ -324,7 +314,9 @@
     )
 
 
-def collect_kernel(full_ref, edge_ref, own_out, far_out, own, far, send, recv, stage, mate, mate_send, mate_recv):
+def collect_kernel(
+    full_ref, edge_ref, own_out, far_out, own, far, send, recv, stage, mate, mate_send, mate_recv, rows
+):
     core = lax.axis_index("sub")
     margin = far.shape[-1]
     traces = own.shape[-1]
@@ -343,7 +335,7 @@
     far_out[pl.ds(1 - core, 1), :] = mate[1, :, :margin]
 
 
-def share_kernel(full_ref, edge_ref, out_ref, own, far, send, recv, stage, mate, mate_send, mate_recv):
+def share_kernel(full_ref, edge_ref, out_ref, own, far, send, recv, stage, mate, mate_send, mate_recv, rows):
     core = lax.axis_index("sub")
     count = lax.axis_size("wide")
     width = far.shape[-1]
@@ -355,12 +347,15 @@
         stage[slot] = own[slot]
         stage[slot, :, :width] = own[slot, :, :width] + far[slot]
         mate_copy(slot).start()
-        out_ref[pl.ds(2 * slot + core, 1), :] = stage[slot]
+        rows[pl.ds(2 * slot + core, 1), :] = stage[slot]
 
     exchange(1, full_ref, edge_ref, own, far, send, recv, consume)
     for slot in range(count):
         mate_copy(slot).wait()
-        out_ref[pl.ds(2 * slot + 1 - core, 1), :] = mate[slot]
+        rows[pl.ds(2 * slot + 1 - core, 1), :] = mate[slot]
+    exact = rows[...]
+    high = exact.astype(jnp.bfloat16).astype(jnp.float32)
+    out_ref[...] = jnp.concatenate([high, high, exact - high], 0).astype(jnp.bfloat16)
 
 
 def exchange_call(kernel, name, full, edge, outs, slots, identity):
@@ -369,7 +364,7 @@
     return pl.pallas_call(
         kernel,
         name=name,
-        out_shape=[jax.ShapeDtypeStruct(o, jnp.float32) for o in outs],
+        out_shape=[jax.ShapeDtypeStruct(*o) for o in outs],
         in_specs=[pl.BlockSpec(memory_space=pltpu.VMEM)] * 2,
         out_specs=[pl.BlockSpec(memory_space=pltpu.VMEM)] * len(outs),
         scratch_shapes=[
@@ -381,6 +376,7 @@
             pltpu.VMEM((slots, 1, traces), jnp.float32),
             pltpu.SemaphoreType.DMA((slots,)),
             pltpu.SemaphoreType.DMA((slots,)),
+            pltpu.VMEM((2 * slots, traces), jnp.float32),
         ],
         compiler_params=pltpu.CompilerParams(
             collective_id=identity, has_side_effects=True, vmem_limit_bytes=40 * 1024 * 1024
@@ -396,12 +392,14 @@
     freq_total = FD * wide_count
     traces = plane_count * TR3
     margin = (LH - 1) * TR3
-    forward = forward_table(time_total, freq_total)
+    forward, inverse = (jnp.asarray(table) for table in tables(time_total, freq_total))
     own_forward = lax.dynamic_slice_in_dim(forward, mine * time_local, time_local, 1)
-    partial = jnp.dot(own_forward, survey.reshape(time_local, traces), preferred_element_type=jnp.float32)
+    partial = lax.dot_general(
+        own_forward, survey, (((1,), (0,)), ((), ())), preferred_element_type=jnp.float32
+    )
     partial = partial.reshape(2 * freq_total, 1, traces)
     spectra, rim = exchange_call(
-        collect_kernel, "collect", partial, partial[:, :, :margin], [(2 * FD, traces), (2 * FD, margin)], 2, 0
+        collect_kernel, "collect", partial, partial[:, :, :margin], [((2 * FD, traces), jnp.float32), ((2 * FD, margin), jnp.float32)], 2, 0
     )
     grid = jnp.concatenate([spectra, rim], 1).reshape(FD, 2, PS, PS, PLANE)
     test_rows = jnp.pad(
@@ -414,20 +412,17 @@
         "share",
         smooth[:, :, :traces],
         smooth[:, :, traces:],
-        [(2 * freq_total, traces)],
+        [((6 * freq_total, traces), jnp.bfloat16)],
         wide_count,
         1,
     )
-    inverse = inverse_table(time_total, freq_total)
     own_inverse = lax.dynamic_slice_in_dim(inverse, mine * time_local, time_local, 1)
-    series = lax.dot_general(
+    return lax.dot_general(
         own_inverse,
-        gathered,
+        gathered.reshape(6 * freq_total, plane_count, TR3),
         (((0,), (0,)), ((), ())),
-        precision=HIGHEST,
         preferred_element_type=jnp.float32,
     )
-    return series.reshape(time_local, plane_count, TR3)
 
 
 def solution(mesh):

time: 45.4 us -> 42.8 us (0.943)
  local copies, waits for them, and re-layouts: 4.62 us -> 2.37 us
    reshape x3 -> x1, local copies, waits for them, and re-layouts: 2.89 us -> 0.32 us  [shards(): gathered.reshape(6 * freq_total, plane_count, TR3)]
where the time goes in v4:
time: 42.8 us; the launch traced here: 42.6 us
  Pallas kernels  36.5 us (85%)
  matrix products  3.53 us (8%)
  local copies, waits for them, and re-layouts  2.37 us (6%)
    pallas_call x2, Pallas kernels, exchange_call(): pl.pallas_call(kernel, name=name, out_shape=[jax.ShapeDtypeStruct(*o) for...  19.2 us
    pallas_call x1, Pallas kernels, reduce_frequency(): pl.pallas_call(frequency_kernel, name='frequency', out_shape=jax.ShapeDty...  17.3 us
    dot_general x1, matrix products, shards(): lax.dot_general(own_inverse, gathered.reshape(6 * freq_total, plane_count...  2.43 us
    dot_general x1, matrix products, shards(): lax.dot_general(own_forward, survey, (((1,), (0,)), ((), ())), preferred_...  1.1 us
    reshape x1, local copies, waits for them, and re-layouts, shards(): test_matrix.T.reshape(RANK, LH, LH * INNER)  1.07 us

profile of v4, /device:TPU:0, one launch (start us, length us, event | category | flops | bytes accessed | tf_op | source)
XLA Modules:
  0.0 42.6 jit_solution(13947434430606482381)
XLA Ops:
  0.0 0.0 copy-start
  0.0 0.0 copy-start.3
  0.0 0.0 copy-start.1
  0.0 0.0 copy-start.2
  0.0 1.1 %reshape.20 = bf16[48,5,125]{2,1,0:T(8,128)(2,1)S(1)} reshape(bf16[48,625]{1,0:T(8,128)(2,1)} %bitcast.22) | data formatting | bytes 120000 | tf_op jit(solution)/shard_map/reshape | solution.py:406
  1.1 0.1 copy-done
  1.2 1.1 %fusion.4 = f32[8,5,729]{2,0,1:T(8,128)S(1)} fusion(bf16[128,5,729]{0,2,1:T(8,128)(2,1)S(1)} %copy-done, bf16[8,512]{1,0:T(8,128)(2,1)} %constant.25.clone, s32[]{:T(128)S(6)} %select_n.4), kind=kOutput, calls=%fused_computation.6 | convolution fusion | flops 7464960 | bytes 1051812 | tf_op jit(solution)/shard_map/dot_general | solution.py:397
  2.3 0.1 copy.12
  2.4 0.2 reshape.26.full_ref
  2.6 10.6 %collect.1 = (f32[2,3645]{1,0:T(2,128)S(1)}, f32[2,2916]{1,0:T(2,128)S(1)}) custom-call(f32[8,1,3645]{2,1,0:T(1,128)S(1)} %reshape.26.full_ref, f32[8,1,2916]{2,1,0:T(1,128)S(1)} %slice.16.edge_ref), custom_call_target="tpu_custom_call" | custom-call | tf_op jit(solution)/shard_map/collect/pallas_call | solution.py:364
  13.2 0.1 pad_maximum_fusion
  13.3 0.2 squeeze_reshape.3
  13.5 0.0 copy-done.3
  13.5 0.0 copy-done.1
  13.5 0.0 copy-done.2
  13.6 17.3 %frequency.1 = f32[9,18,128]{2,1,0:T(8,128)S(1)} custom-call(f32[9,18,128]{2,1,0:T(8,128)S(1)} %pad.8.x_ref, bf16[48,640]{1,0:T(8,128)(2,1)S(1)} %bitcast.18, bf16[640,128]{1,0:T(8,128)(2,1)S(1)} %copy-done.2, bf16[256,640]{1,0:T(8,128)(2,1)S(1)} %copy-done.1, f32[9,18,128]{2,1,0:T(8,128)S(1)} %copy-done.3), custom_call_target="tpu_custom_call" | custom-call | tf_op jit(solution)/shard_map/frequency/pallas_call | solution.py:221
  30.9 0.1 copy.16
  31.0 0.2 reshape_stack_reshape.4
  31.2 0.1 slice.19.edge_ref
  31.3 8.6 %share.1 = bf16[24,3645]{1,0:T(8,128)(2,1)S(1)} custom-call(f32[2,1,3645]{2,1,0:T(1,128)S(1)} %slice.18.full_ref, f32[2,1,2916]{2,1,0:T(1,128)S(1)} %slice.19.edge_ref), custom_call_target="tpu_custom_call" | custom-call | tf_op jit(solution)/shard_map/share/pallas_call | solution.py:364
  39.9 0.3 reshape.23
  40.2 2.4 %fusion = f32[128,5,729]{0,2,1:T(8,128)} fusion(bf16[24,5,729]{2,1,0:T(8,128)(2,1)S(1)} %reshape.23, bf16[24,512]{1,0:T(8,128)(2,1)} %constant.26.clone, s32[]{:T(128)S(6)} %select_n.4), kind=kOutput, calls=%fused_computation | convolution fusion | flops 22394880 | bytes 2047348 | tf_op jit(solution)/shard_map/dot_general | solution.py:420
  (7 shorter events, 0.1 us)
Async XLA Ops:
  0.0 1.2 %copy-start = (bf16[128,5,729]{0,2,1:T(8,128)(2,1)S(1)}, bf16[128,5,729]{0,2,1:T(8,128)(2,1)}, u32[]{:S(2)}) copy-start(bf16[128,5,729]{0,2,1:T(8,128)(2,1)} %param.7) | copy-start | bytes 2799364
  0.0 13.5 %copy-start.3 = (f32[9,18,128]{2,1,0:T(8,128)S(1)}, f32[9,18,128]{2,1,0:T(8,128)}, u32[]{:S(2)}) copy-start(f32[9,18,128]{2,1,0:T(8,128)} %constant.29.clone.scale_ref) | copy-start | bytes 248836
  0.0 13.5 %copy-start.1 = (bf16[256,640]{1,0:T(8,128)(2,1)S(1)}, bf16[256,640]{1,0:T(8,128)(2,1)}, u32[]{:S(2)}) copy-start(bf16[256,640]{1,0:T(8,128)(2,1)} %constant.28.clone.pick_t_ref) | copy-start | bytes 983044
  0.0 13.5 %copy-start.2 = (bf16[640,128]{1,0:T(8,128)(2,1)S(1)}, bf16[640,128]{1,0:T(8,128)(2,1)}, u32[]{:S(2)}) copy-start(bf16[640,128]{1,0:T(8,128)(2,1)} %constant.27.clone.pick_ref) | copy-start | bytes 491524
